TPU v7x, 512 devices: a whole 4x8x8 slice. The times are simulated.
512 devices in a mesh: grp: 32 (over y, z_hi, core), leaf: 16 (over z_lo, x).
Axes of the slice: x: 4, y: 8, z: 8 (z_hi: 2, z_lo: 4; z = z_hi * 4 + z_lo), core: 2. Of those that a mesh axis runs over, the one named last changes fastest.
Arguments:
- vectors: bfloat16 [32, 2097152], P(None, ('grp', 'leaf')), may hold values from -6 to 6
- offsets: bfloat16 [3, 2097152], P(None, ('grp', 'leaf')), may hold values from 0 to 1
- near_list: int32 [8192, 16], P(('grp', 'leaf')), may hold values from 0 to 8191, as said below
- near_count: int32 [8192], P(('grp', 'leaf')), may hold values from 8 to 16, as said below
- leaf_basis: bfloat16 [8192, 64, 256], P(('grp', 'leaf')), may hold values from -0.375 to 0.375
- far_list: int32 [8192, 16], P(('grp', 'leaf')), may hold values from 0 to 8191, as said below
- far_count: int32 [8192], P(('grp', 'leaf')), may hold values from 0 to 16, as said below
- leaf_coupling: bfloat16 [8192, 16, 64, 64], P(('grp', 'leaf')), as said below
- transfer: bfloat16 [8192, 64, 64], P(('grp', 'leaf')), may hold values from -0.75 to 0.75
- group_list: int32 [32, 16], P('grp'), may hold values from 0 to 31, as said below
- group_count: int32 [32], P('grp'), may hold values from 8 to 16, as said below
- group_coupling: bfloat16 [32, 16, 64, 64], P('grp', 'leaf'), may hold values from -0.01171875 to 0.01171875
Outputs:
- applied: bfloat16 [32, 2097152], P(None, ('grp', 'leaf'))
Inputs may be any that keep to these rules, and one draw needn't show every extreme that they name: `near_list`: the first near_count[l] entries of row l are distinct leaves of l's own group lying on l's device or on the devices just before and after it along leaf (16 consecutive leaves a device); the first entry is l itself and the remaining entries repeat l. `near_count`: the first leaf of every device has exactly 16. `far_list`: the first far_count[l] entries of row l are distinct leaves of l's own group other than l; the remaining entries repeat l. If leaf j stands in slot k < far_count[l] of row l, then l stands in some slot k2 < far_count[j] of row j. `far_count`: the first leaf of every group has exactly 16. If far_list[l, k] = j with k < far_count[l], and far_list[j, k2] = l with k2 < far_count[j], then leaf_coupling[j, k2] is the transpose of leaf_coupling[l, k]. `group_list`: the first group_count[g] entries of row g are distinct groups other than g; the remaining entries repeat g. `group_count`: group 0 has exactly 16.
All inputs are finite; a program needn't handle non-finite values.
Results may differ from a plain program's by a relative error of at most 0.005.
Values may be sent and summed in bfloat16 or wider, within the bound.
No kernel may reach another device: no remote copies, remote signals or barrier semaphores. Data moves between devices by JAX's collectives and lax.ppermute only.
A program may use at most 64 MiB of HBM per device.

v0:
```python
import jax
import jax.numpy as jnp
from jax import lax
from jax.sharding import PartitionSpec as P

inv_four_pi = 0.07957747154594767
soften = 0.01


def with_halo(shard, sides, width):
    for axis, dim in sides:
        count, length = (lax.axis_size(axis), shard.shape[dim])
        up = [(i, (i + 1) % count) for i in range(count - 1)]
        down = [(j, i) for i, j in up]
        last = lax.slice_in_dim(shard, length - width, length, axis=dim)
        first = lax.slice_in_dim(shard, 0, width, axis=dim)
        before = lax.ppermute(last, axis, up)
        after = lax.ppermute(first, axis, down)
        shard = jnp.concatenate([before, shard, after], axis=dim)
    return shard


def centres(leaf_ids):
    columns = []
    for axis_pos in range(3):
        summed = jnp.zeros_like(leaf_ids)
        for bit_pos in range(10):
            picked = jnp.bitwise_and(jnp.right_shift(leaf_ids, 3 * bit_pos + axis_pos), 1)
            summed = summed + jnp.left_shift(picked, bit_pos)
        columns.append(summed.astype(jnp.float32))
    return jnp.stack(columns)


def kernel_tile(source_pts, target_pts):
    squared = jnp.zeros(
        (source_pts.shape[0], source_pts.shape[2], target_pts.shape[1]), jnp.float32
    )
    for axis_pos in range(3):
        spacing = source_pts[:, axis_pos, :, None] - target_pts[axis_pos][None, None, :]
        squared = squared + spacing * spacing
    return inv_four_pi * lax.rsqrt(squared + soften)


def body(
    vectors,
    offsets,
    near_list,
    near_count,
    leaf_basis,
    far_list,
    far_count,
    leaf_coupling,
    transfer,
    group_list,
    group_count,
    group_coupling,
):
    leaf_devices = lax.axis_size("leaf")
    local_leaves = near_list.shape[0]
    near_slots = near_list.shape[1]
    far_slots = far_list.shape[1]
    vec_count = vectors.shape[0]
    leaf_width = vectors.shape[1] // local_leaves
    group_leaves = leaf_devices * local_leaves
    leaf_place = lax.axis_index("leaf")
    group_place = lax.axis_index("grp")
    device_first = (group_place * leaf_devices + leaf_place) * local_leaves
    group_first = group_place * group_leaves
    window_first = device_first - local_leaves
    stacked = jnp.concatenate([vectors, offsets], axis=0)
    widened = with_halo(stacked, (("leaf", 1),), local_leaves * leaf_width)
    window_vectors = widened[:vec_count].reshape(vec_count, 3 * local_leaves, leaf_width)
    window_ids = window_first + jnp.arange(3 * local_leaves, dtype=jnp.int32)
    window_pts = (
        widened[vec_count:].astype(jnp.float32).reshape(3, 3 * local_leaves, leaf_width)
        + centres(window_ids)[:, :, None]
    )
    slot_ids = jnp.arange(near_slots, dtype=jnp.int32)

    def near_step(running, target):
        sources = near_list[target] - window_first
        active_slots = slot_ids < near_count[target]
        source_pts = jnp.take(window_pts, sources, axis=1).transpose(1, 0, 2)
        target_pts = lax.dynamic_index_in_dim(window_pts, local_leaves + target, 1, keepdims=False)
        near_tile = jnp.where(
            active_slots[:, None, None], kernel_tile(source_pts, target_pts), 0.0
        ).astype(jnp.bfloat16)
        source_vectors = jnp.take(window_vectors, sources, axis=1)
        return (
            running,
            jnp.einsum(
                "vkb,kba->va", source_vectors, near_tile, preferred_element_type=jnp.float32
            ),
        )

    ignored, near_field = lax.scan(near_step, 0, jnp.arange(local_leaves, dtype=jnp.int32))
    leaf_vectors = vectors.reshape(vec_count, local_leaves, leaf_width)
    coeffs = jnp.einsum(
        "via,ira->ivr", leaf_vectors, leaf_basis, preferred_element_type=jnp.float32
    ).astype(jnp.bfloat16)
    far_active = jnp.arange(far_slots, dtype=jnp.int32)[None, :] < far_count[:, None]
    far_rows = far_list - group_first
    group_coeffs = lax.all_gather(coeffs, "leaf", axis=0, tiled=True)
    picked = jnp.take(group_coeffs, far_rows, axis=0)
    picked = jnp.where(far_active[:, :, None, None], picked, jnp.zeros((), jnp.bfloat16))
    far_field = jnp.einsum(
        "ikvs,ikrs->ivr", picked, leaf_coupling, preferred_element_type=jnp.float32
    )
    coarse_part = jnp.einsum("ivs,isr->vr", coeffs, transfer, preferred_element_type=jnp.float32)
    coarse = lax.psum(coarse_part, "leaf").astype(jnp.bfloat16)
    all_coarse = lax.all_gather(coarse[None], "grp", axis=0, tiled=True)
    group_active = jnp.arange(group_list.shape[1], dtype=jnp.int32) < group_count[0]
    own_slots = group_coupling.shape[1]
    slot_first = leaf_place * own_slots
    own_groups = lax.dynamic_slice_in_dim(group_list[0], slot_first, own_slots, 0)
    own_active = lax.dynamic_slice_in_dim(group_active, slot_first, own_slots, 0)
    picked_groups = jnp.where(
        own_active[:, None, None],
        jnp.take(all_coarse, own_groups, axis=0),
        jnp.zeros((), jnp.bfloat16),
    )
    coarse_term = jnp.einsum(
        "kvs,krs->vr", picked_groups, group_coupling[0], preferred_element_type=jnp.float32
    )
    coarse_out = lax.psum(coarse_term, "leaf")
    downward = jnp.einsum(
        "vs,irs->ivr", coarse_out.astype(jnp.bfloat16), transfer, preferred_element_type=jnp.float32
    )
    local_coeffs = (far_field + downward).astype(jnp.bfloat16)
    expanded = jnp.einsum(
        "ivr,ira->via", local_coeffs, leaf_basis, preferred_element_type=jnp.float32
    )
    result = jnp.transpose(near_field, (1, 0, 2)) + expanded
    return result.reshape(vec_count, local_leaves * leaf_width).astype(jnp.bfloat16)


def solution(mesh):
    placed = (
        P(None, ("grp", "leaf")),
        P(None, ("grp", "leaf")),
        P(("grp", "leaf"), None),
        P(("grp", "leaf")),
        P(("grp", "leaf"), None, None),
        P(("grp", "leaf"), None),
        P(("grp", "leaf")),
        P(("grp", "leaf"), None, None, None),
        P(("grp", "leaf"), None, None),
        P("grp", None),
        P("grp"),
        P("grp", "leaf", None, None),
    )
    return jax.shard_map(
        body, mesh=mesh, in_specs=placed, out_specs=P(None, ("grp", "leaf")), check_vma=False
    )
```

profile of v0, /device:TPU:8, one launch (start us, length us, event | category | flops | bytes accessed | tf_op | source)
XLA Modules:
  0.0 398.0 jit_solution(17522042291182980777)
XLA Ops:
  6.5 1.0 constant_dynamic-update-slice_fusion.1
  7.6 0.8 constant_dynamic-update-slice_fusion
  8.4 1.3 collective-permute-start.1
  9.7 4.6 %collective-permute-start = (bf16[35,4096]{1,0:T(8,128)(2,1)S(1)}, bf16[35,4096]{1,0:T(8,128)(2,1)S(1)}, u32[]{:S(2)}, u32[]{:S(2)}) collective-permute-start(bf16[35,4096]{1,0:T(8,128)(2,1)S(1)} %constant_dynamic-update-slice_fusion), channel_id=1, source_target_pairs={{0,1},{1,2},{2,3},{3,4},{4,5},{5,6},{6,7},{7,8},{8,9},{9,10},{10,1... | collective-permute-start | bytes 860168 | tf_op jit(solution)/shard_map/ppermute | solution.py:17
  14.3 1.9 convolution_convert_fusion
  17.5 1.2 constant_dynamic-slice_fusion.4
  21.3 1.2 convolution_bitcast_fusion.1
  22.5 80.5 %psum.14 = bf16[32,64]{1,0:T(8,128)(2,1)S(1)} all-reduce(f32[32,64]{1,0:T(8,128)S(1)} %convolution_bitcast_fusion.1), channel_id=1, replica_groups=mesh['grp'=32,'leaf'=16] {'leaf'}, use_global_device_ids=true, to_apply=%region_2.3 | all-reduce | flops 2048 | bytes 12288 | tf_op jit(solution)/shard_map/psum | solution.py:110
  103.0 53.7 %all-gather = bf16[1024,64]{1,0:T(8,128)(2,1)S(1)} all-gather(bf16[32,64]{1,0:T(8,128)(2,1)S(1)} %psum.14), channel_id=2, replica_groups=mesh['grp'=32,'leaf'=16] {'grp'}, dimensions={0}, use_global_device_ids=true | all-gather | bytes 135168 | tf_op jit(solution)/shard_map/all_gather | solution.py:111
  156.7 1.5 fusion.30
  158.2 74.2 %psum.15 = bf16[32,64]{1,0:T(8,128)(2,1)S(1)} all-reduce(f32[32,64]{1,0:T(8,128)S(1)} %fusion.30), channel_id=1, replica_groups=mesh['grp'=32,'leaf'=16] {'leaf'}, use_global_device_ids=true, to_apply=%region_3.4 | all-reduce | flops 2048 | bytes 12288 | tf_op jit(solution)/shard_map/psum | solution.py:125
  232.5 0.7 iota_compare_fusion
  233.6 148.9 %while.15 = (s32[]{:T(128)}, f32[16,32,256]{2,1,0:T(8,128)S(1)}, s32[16]{0:T(128)S(1)}, s32[16,16]{1,0:T(8,128)}, s32[]{:T(128)}, /*index=5*/bf16[32,48,256]{2,0...) while((s32[]{:T(128)}, f32[16,32,256]{2,1,0:T(8,128)S(1)}, ...), condition=%wide.region_1.2_spmd.clone, body=%wide.region_0.1_spmd.clone.sunk | while | flops 79836360 | bytes 1276693 | solution.py:96
  238.3 1.4 compare_and_fusion.3
  241.1 1.9 fusion.62
  247.7 1.4 compare_and_fusion.3
  250.4 1.9 fusion.62
  257.0 1.4 compare_and_fusion.3
  259.7 1.9 fusion.62
  266.3 1.4 compare_and_fusion.3
  269.0 1.9 fusion.62
  275.6 1.4 compare_and_fusion.3
  278.3 1.9 fusion.62
  284.9 1.4 compare_and_fusion.3
  287.6 1.9 fusion.62
  294.2 1.4 compare_and_fusion.3
  296.9 1.9 fusion.62
  303.5 1.4 compare_and_fusion.3
  306.2 1.9 fusion.62
  312.8 1.4 compare_and_fusion.3
  315.6 1.9 fusion.62
  322.1 1.4 compare_and_fusion.3
  324.9 1.9 fusion.62
  331.4 1.4 compare_and_fusion.3
  334.2 1.9 fusion.62
  340.7 1.4 compare_and_fusion.3
  343.5 1.9 fusion.62
  350.0 1.4 compare_and_fusion.3
  352.8 1.9 fusion.62
  359.3 1.4 compare_and_fusion.3
  362.1 1.9 fusion.62
  368.7 1.4 compare_and_fusion.3
  371.4 1.9 fusion.62
  378.0 1.4 compare_and_fusion.3
  380.7 1.9 fusion.62
  382.6 2.6 gather_fusion.2
  385.2 3.8 fusion.20
  389.0 1.4 fusion.23
  (220 shorter events, 55.7 us)
Async XLA Ops:
  6.5 7.7 %copy-start = (bf16[16,64,256]{2,1,0:T(8,128)(2,1)S(1)}, bf16[16,64,256]{2,1,0:T(8,128)(2,1)}, u32[]{:S(2)}) copy-start(bf16[16,64,256]{2,1,0:T(8,128)(2,1)} %param.18) | copy-start | bytes 1572868
  6.5 376.0 %all-gather.3.cloned.1.call-start = ((), (), s32[]{:S(2)}) async-start(), calls=%async_computation | async-start | bytes 2228224 | tf_op jit(solution)/shard_map/all_gather | solution.py:103
  8.4 224.9 %collective-permute-start.1 = (bf16[35,4096]{1,0:T(8,128)(2,1)S(1)}, bf16[35,4096]{1,0:T(8,128)(2,1)S(1)}, u32[]{:S(2)}, u32[]{:S(2)}) collective-permute-start(bf16[35,4096]{1,0:T(8,128)(2,1)S(1)} %constant_dynamic-update-slice_fusion), channel_id=1, source_target_pairs={{1,0},{2,1},{3,2},{4,3},{5,4},{6,5},{7,6},{8,7},{9,8},{10,9},{11,1... | collective-permute-start | bytes 860168 | tf_op jit(solution)/shard_map/ppermute | solution.py:18
  9.7 223.6 %collective-permute-start = (bf16[35,4096]{1,0:T(8,128)(2,1)S(1)}, bf16[35,4096]{1,0:T(8,128)(2,1)S(1)}, u32[]{:S(2)}, u32[]{:S(2)}) collective-permute-start(bf16[35,4096]{1,0:T(8,128)(2,1)S(1)} %constant_dynamic-update-slice_fusion), channel_id=1, source_target_pairs={{0,1},{1,2},{2,3},{3,4},{4,5},{5,6},{6,7},{7,8},{8,9},{9,10},{10,1... | collective-permute-start | bytes 860168 | tf_op jit(solution)/shard_map/ppermute | solution.py:17
  14.2 219.4 %copy-start.2 = (s32[16]{0:T(128)S(1)}, s32[16]{0:T(128)}, u32[]{:S(2)}) copy-start(s32[16]{0:T(128)} %param.17) | copy-start | bytes 196
  385.2 3.8 copy-start.1
Sparse Core Ops, SparseCore 0:
  16.3 92.5 all-gather.2
where the time goes:
time: 400 us; the launch traced here: 398 us
  blocking collectives  208 us (52%)
  local copies, waits for them, and re-layouts  47.7 us (12%)
  loops' own time  44.3 us (11%)
  matrix products  39.6 us (10%)
  other arithmetic  36.2 us (9%)
  between operations  15.9 us (4%)
  starting transfers between devices  5.86 us (1%)
    psum x1, blocking collectives, body(): coarse = lax.psum(coarse_part, 'leaf').astype(jnp.bfloat16)  80.5 us
    psum x1, blocking collectives, body(): coarse_out = lax.psum(coarse_term, 'leaf')  74.2 us
    all_gather x1, blocking collectives, body(): all_coarse = lax.all_gather(coarse[None], 'grp', axis=0, tiled=True)  53.7 us
    another operation x1, loops' own time, body(): lax.scan(near_step, 0, jnp.arange(local_leaves, dtype=jnp.int32))  44.3 us
    dot_general x16, matrix products, near_step(): jnp.einsum('vkb,kba->va', source_vectors, near_tile, preferred_element_ty...  29.8 us
    and x16, other arithmetic, near_step(): source_vectors = jnp.take(window_vectors, sources, axis=1)  21.9 us
    select_n x16, other arithmetic, near_step(): source_vectors = jnp.take(window_vectors, sources, axis=1)  11.1 us
    dynamic_slice x16, local copies, waits for them, and re-layouts, body(): lax.scan(near_step, 0, jnp.arange(local_leaves, dtype=jnp.int32))  10.5 us
  transfers between devices with their start and end apart: 3, of which 0 were waited for; matrix products, arithmetic and copies ran while one was open for 28% of the time, Pallas kernels for 0%

commit v1 on v0

--- a/solution.py
+++ b/solution.py
@@ -122,7 +122,7 @@
     coarse_term = jnp.einsum(
         "kvs,krs->vr", picked_groups, group_coupling[0], preferred_element_type=jnp.float32
     )
-    coarse_out = lax.psum(coarse_term, "leaf")
+    coarse_out = jnp.sum(lax.all_gather(coarse_term, "leaf"), axis=0)
     downward = jnp.einsum(
         "vs,irs->ivr", coarse_out.astype(jnp.bfloat16), transfer, preferred_element_type=jnp.float32
     )

time: 400 us -> 367 us (0.917)
  the two profiles are of different devices: /device:TPU:8 before, /device:TPU:2 now
where the time goes in v1:
time: 367 us; the launch traced here: 365 us
  blocking collectives  171 us (47%)
  local copies, waits for them, and re-layouts  47.7 us (13%)
  loops' own time  44.3 us (12%)
  matrix products  39.7 us (11%)
  other arithmetic  36.3 us (10%)
  between operations  15.9 us (4%)
  starting transfers between devices  9.74 us (3%)
    psum x1, blocking collectives, body(): coarse = lax.psum(coarse_part, 'leaf').astype(jnp.bfloat16)  72.3 us
    all_gather x1, blocking collectives, body(): all_coarse = lax.all_gather(coarse[None], 'grp', axis=0, tiled=True)  54.6 us
    all_gather x1, blocking collectives, body(): coarse_out = jnp.sum(lax.all_gather(coarse_term, 'leaf'), axis=0)  44.3 us
    another operation x1, loops' own time, body(): lax.scan(near_step, 0, jnp.arange(local_leaves, dtype=jnp.int32))  44.3 us
    dot_general x16, matrix products, near_step(): jnp.einsum('vkb,kba->va', source_vectors, near_tile, preferred_element_ty...  29.8 us
    and x16, other arithmetic, near_step(): source_vectors = jnp.take(window_vectors, sources, axis=1)  22 us
    select_n x16, other arithmetic, near_step(): source_vectors = jnp.take(window_vectors, sources, axis=1)  11.1 us
    dynamic_slice x16, local copies, waits for them, and re-layouts, body(): lax.scan(near_step, 0, jnp.arange(local_leaves, dtype=jnp.int32))  10.5 us
  transfers between devices with their start and end apart: 3, of which 0 were waited for; matrix products, arithmetic and copies ran while one was open for 31% of the time, Pallas kernels for 0%

profile of v1, /device:TPU:2, one launch (start us, length us, event | category | flops | bytes accessed | tf_op | source)
XLA Modules:
  0.0 364.7 jit_solution(16499446873418673432)
XLA Ops:
  6.5 1.0 constant_dynamic-update-slice_fusion.1
  7.6 0.8 constant_dynamic-update-slice_fusion
  8.4 7.8 %collective-permute-start.1 = (bf16[35,4096]{1,0:T(8,128)(2,1)S(1)}, bf16[35,4096]{1,0:T(8,128)(2,1)S(1)}, u32[]{:S(2)}, u32[]{:S(2)}) collective-permute-start(bf16[35,4096]{1,0:T(8,128)(2,1)S(1)} %constant_dynamic-update-slice_fusion), channel_id=1, source_target_pairs={{1,0},{2,1},{3,2},{4,3},{5,4},{6,5},{7,6},{8,7},{9,8},{10,9},{11,1... | collective-permute-start | bytes 860168 | tf_op jit(solution)/shard_map/ppermute | solution.py:18
  16.2 1.9 collective-permute-start
  18.1 1.9 convolution_convert_fusion
  21.4 1.2 constant_dynamic-slice_fusion.4
  25.2 1.2 convolution_bitcast_fusion.1
  26.4 72.3 %psum.7 = bf16[32,64]{1,0:T(8,128)(2,1)S(1)} all-reduce(f32[32,64]{1,0:T(8,128)S(1)} %convolution_bitcast_fusion.1), channel_id=1, replica_groups=mesh['grp'=32,'leaf'=16] {'leaf'}, use_global_device_ids=true, to_apply=%region_2.3 | all-reduce | flops 2048 | bytes 12288 | tf_op jit(solution)/shard_map/psum | solution.py:110
  98.7 54.6 %all-gather = bf16[1024,64]{1,0:T(8,128)(2,1)S(1)} all-gather(bf16[32,64]{1,0:T(8,128)(2,1)S(1)} %psum.7), channel_id=2, replica_groups=mesh['grp'=32,'leaf'=16] {'grp'}, dimensions={0}, use_global_device_ids=true | all-gather | bytes 135168 | tf_op jit(solution)/shard_map/all_gather | solution.py:111
  153.3 1.5 fusion.30
  154.8 44.3 %all-gather.1 = f32[512,64]{1,0:T(8,128)S(1)} all-gather(f32[32,64]{1,0:T(8,128)S(1)} %fusion.30), channel_id=3, replica_groups=mesh['grp'=32,'leaf'=16] {'leaf'}, dimensions={0}, use_global_device_ids=true | all-gather | bytes 139264 | tf_op jit(solution)/shard_map/all_gather | solution.py:125
  199.1 0.7 iota_compare_fusion
  200.3 148.9 %while.15 = (s32[]{:T(128)}, f32[16,32,256]{2,1,0:T(8,128)S(1)}, s32[16]{0:T(128)S(1)}, s32[16,16]{1,0:T(8,128)}, s32[]{:T(128)}, /*index=5*/bf16[32,48,256]{2,0...) while((s32[]{:T(128)}, f32[16,32,256]{2,1,0:T(8,128)S(1)}, ...), condition=%wide.region_1.2_spmd.clone, body=%wide.region_0.1_spmd.clone.sunk | while | flops 79836360 | bytes 1276693 | solution.py:96
  205.0 1.4 compare_and_fusion.3
  207.8 1.9 fusion.62
  214.3 1.4 compare_and_fusion.3
  217.1 1.9 fusion.62
  223.6 1.4 compare_and_fusion.3
  226.4 1.9 fusion.62
  232.9 1.4 compare_and_fusion.3
  235.7 1.9 fusion.62
  242.2 1.4 compare_and_fusion.3
  245.0 1.9 fusion.62
  251.5 1.4 compare_and_fusion.3
  254.3 1.9 fusion.62
  260.9 1.4 compare_and_fusion.3
  263.6 1.9 fusion.62
  270.2 1.4 compare_and_fusion.3
  272.9 1.9 fusion.62
  279.5 1.4 compare_and_fusion.3
  282.2 1.9 fusion.62
  288.8 1.4 compare_and_fusion.3
  291.5 1.9 fusion.62
  298.1 1.4 compare_and_fusion.3
  300.8 1.9 fusion.62
  307.4 1.4 compare_and_fusion.3
  310.1 1.9 fusion.62
  316.7 1.4 compare_and_fusion.3
  319.4 1.9 fusion.62
  326.0 1.4 compare_and_fusion.3
  328.8 1.9 fusion.62
  335.3 1.4 compare_and_fusion.3
  338.1 1.9 fusion.62
  344.6 1.4 compare_and_fusion.3
  347.4 1.9 fusion.62
  349.2 2.6 gather_fusion.2
  351.8 3.8 %fusion.20 = f32[16,32,64]{2,1,0:T(8,128)} fusion(bf16[16,16,64,64]{3,2,1,0:T(8,128)(2,1)} %param.21, bf16[16,16,32,64]{3,2,1,0:T(8,128)(2,1)S(1)} %bitcast.108, pred[16,16]{1,0:T(8,128)(4,1)S(1)} %get-tuple-element.195, pred[16,16]{1,0:T(8,128)(4,1)S(1)} %iota_compare_fusion), kind=kOutput, calls=%fused_computation.38 | convolution fusion | flops 68157440 | bytes 3277312 | tf_op jit(solution)/shard_map/ikvs,ikrs->ivr/dot_general | solution.py:106
  355.7 1.4 fusion.23
  (221 shorter events, 55.7 us)
Async XLA Ops:
  6.5 11.6 %copy-start = (bf16[16,64,256]{2,1,0:T(8,128)(2,1)S(1)}, bf16[16,64,256]{2,1,0:T(8,128)(2,1)}, u32[]{:S(2)}) copy-start(bf16[16,64,256]{2,1,0:T(8,128)(2,1)} %param.18) | copy-start | bytes 1572868
  6.5 342.7 %all-gather.4.cloned.1.call-start = ((), (), s32[]{:S(2)}) async-start(), calls=%async_computation | async-start | bytes 2228224 | tf_op jit(solution)/shard_map/all_gather | solution.py:103
  8.4 191.5 %collective-permute-start.1 = (bf16[35,4096]{1,0:T(8,128)(2,1)S(1)}, bf16[35,4096]{1,0:T(8,128)(2,1)S(1)}, u32[]{:S(2)}, u32[]{:S(2)}) collective-permute-start(bf16[35,4096]{1,0:T(8,128)(2,1)S(1)} %constant_dynamic-update-slice_fusion), channel_id=1, source_target_pairs={{1,0},{2,1},{3,2},{4,3},{5,4},{6,5},{7,6},{8,7},{9,8},{10,9},{11,1... | collective-permute-start | bytes 860168 | tf_op jit(solution)/shard_map/ppermute | solution.py:18
  16.2 183.7 %collective-permute-start = (bf16[35,4096]{1,0:T(8,128)(2,1)S(1)}, bf16[35,4096]{1,0:T(8,128)(2,1)S(1)}, u32[]{:S(2)}, u32[]{:S(2)}) collective-permute-start(bf16[35,4096]{1,0:T(8,128)(2,1)S(1)} %constant_dynamic-update-slice_fusion), channel_id=1, source_target_pairs={{0,1},{1,2},{2,3},{3,4},{4,5},{5,6},{6,7},{7,8},{8,9},{9,10},{10,1... | collective-permute-start | bytes 860168 | tf_op jit(solution)/shard_map/ppermute | solution.py:17
  20.0 180.3 %copy-start.2 = (s32[16]{0:T(128)S(1)}, s32[16]{0:T(128)}, u32[]{:S(2)}) copy-start(s32[16]{0:T(128)} %param.17) | copy-start | bytes 196
  351.8 3.8 %copy-start.1 = (bf16[16,64,64]{2,1,0:T(8,128)(2,1)S(1)}, bf16[16,64,64]{2,1,0:T(8,128)(2,1)}, u32[]{:S(2)}) copy-start(bf16[16,64,64]{2,1,0:T(8,128)(2,1)} %param.22) | copy-start | bytes 393220
Sparse Core Ops, SparseCore 0:
  20.1 88.4 all-gather.3
